TPU v7x, 32 devices: a whole 2x2x4 slice. The times are simulated.
32 devices in a mesh: ta: 4 (over x, core), ha: 4 (over z), ga: 2 (over y).
Axes of the slice: x: 2, y: 2, z: 4, core: 2. Of those that a mesh axis runs over, the one named last changes fastest.
Arguments:
- query_in: bfloat16 [12, 4, 8, 8, 512], P('ta', 'ha', None, None, 'ga'), may hold values from -6 to 6
- key_in: bfloat16 [12, 4, 8, 8, 512], P('ta', 'ha', None, None, 'ga'), may hold values from -6.0625 to 6.0625
- value_in: bfloat16 [12, 4, 8, 8, 512], P('ta', 'ha', None, None, 'ga'), may hold values from -6 to 6
- saved_out: bfloat16 [12, 4, 8, 8, 512], P('ta', 'ha', None, None, 'ga'), may hold values from -6 to 6
- out_grad: bfloat16 [12, 4, 8, 8, 512], P('ta', 'ha', None, None, 'ga'), may hold values from -6 to 6
- window_mask: int32 [2, 1, 4, 27], replicated, may hold values from 0 to 1, as said below
Outputs:
- query_grad: bfloat16 [12, 4, 8, 8, 512], P('ta', 'ha', None, None, 'ga')
- key_grad: bfloat16 [12, 4, 8, 8, 512], P('ta', 'ha', None, None, 'ga')
- value_grad: bfloat16 [12, 4, 8, 8, 512], P('ta', 'ha', None, None, 'ga')
Inputs may be any that keep to these rules, and one draw needn't show every extreme that they name: `window_mask`: entry 13 (the tile itself) is 1 for every tile.
All inputs are finite; a program needn't handle non-finite values.
Results may differ from a plain program's by a relative error of at most 0.0058.
Values may be sent and summed in bfloat16 or wider, within the bound.
A program may use at most 128 MiB of HBM per device.

v0:
```python
import jax
import jax.numpy as jnp
from jax import lax
from jax.sharding import PartitionSpec as P

HEAD_DIM = 128
TILE_T = 6


def passed_along(block, axis, distance):
    devices = range(lax.axis_size(axis))
    route = [(i - distance, i) for i in devices if i - distance in devices]
    return lax.ppermute(block, axis, route)


def attend(query_rows, key_rows, value_rows, saved_rows, grad_rows, key_bias, score_scale):
    f32 = jnp.float32
    scores = (
        jnp.einsum("qhd,khd->hqk", query_rows, key_rows, preferred_element_type=f32) * score_scale
        + key_bias[None, None, :]
    )
    row_max = jnp.max(scores, axis=-1, keepdims=True)
    raised = jnp.exp(scores - row_max)
    weights = raised / jnp.sum(raised, axis=-1, keepdims=True)
    weights_low = weights.astype(jnp.bfloat16)
    value_part = jnp.einsum(
        "hqk,qhd->khd", weights_low, grad_rows, preferred_element_type=f32
    ).astype(jnp.bfloat16)
    weight_grad = jnp.einsum("qhd,khd->hqk", grad_rows, value_rows, preferred_element_type=f32)
    row_dot = jnp.einsum("qhd,qhd->hq", grad_rows, saved_rows, preferred_element_type=f32)
    score_grad = (weights * (weight_grad - row_dot[:, :, None]) * score_scale).astype(jnp.bfloat16)
    query_part = jnp.einsum(
        "hqk,khd->qhd", score_grad, key_rows, preferred_element_type=f32
    ).astype(jnp.bfloat16)
    key_part = jnp.einsum(
        "hqk,qhd->khd", score_grad, query_rows, preferred_element_type=f32
    ).astype(jnp.bfloat16)
    return (query_part, key_part, value_part)


def local(query_in, key_in, value_in, saved_out, out_grad, window_mask):
    f32 = jnp.float32
    frames_dev, plane_dev, tile_rows, tile_cols, local_width = query_in.shape
    heads_dev = local_width // HEAD_DIM
    row_tiles = window_mask.shape[1]
    col_tiles = window_mask.shape[2]
    plane_count = lax.axis_size("ha")
    frame_count = frames_dev * lax.axis_size("ta")
    time_index = lax.axis_index("ta")
    plane = lax.axis_index("ha")
    row_tile = plane // col_tiles
    col_tile = plane % col_tiles
    query_time = time_index * frames_dev // TILE_T
    score_scale = HEAD_DIM ** (-0.5)
    neighbours = [(row_move, col_move) for row_move in (-1, 0, 1) for col_move in (-1, 0, 1)]
    own_pair = (key_in[:, 0], value_in[:, 0])
    whole_frames = (
        lax.all_gather(own_pair[0], "ta", axis=0, tiled=True),
        lax.all_gather(own_pair[1], "ta", axis=0, tiled=True),
    )
    received = {(0, 0): whole_frames}
    for surround_row_move, surround_col_move in neighbours:
        if (surround_row_move, surround_col_move) != (0, 0):
            surround_offset = surround_row_move * col_tiles + surround_col_move
            if abs(surround_offset) < plane_count:
                received[surround_row_move, surround_col_move] = passed_along(
                    (whole_frames[0], whole_frames[1]), "ha", -surround_offset
                )
            else:
                received[surround_row_move, surround_col_move] = (
                    jnp.zeros_like(whole_frames[0]),
                    jnp.zeros_like(whole_frames[1]),
                )
    near_keys, near_values = tuple(
        (jnp.stack([received[place][member] for place in neighbours], 0) for member in range(2))
    )
    slot = jnp.arange(9, dtype=jnp.int32)
    row_step = slot // 3 - 1
    col_step = slot % 3 - 1
    time_step = jnp.arange(frame_count, dtype=jnp.int32) // TILE_T - query_time
    code = (time_step[None, :] + 1) * 9 + slot[:, None]
    window_row = (
        lax.dynamic_slice(window_mask, (query_time, row_tile, col_tile, 0), (1, 1, 1, 27))
        .reshape(27)
        .astype(f32)
    )
    matched = (code.reshape(-1)[:, None] == jnp.arange(27, dtype=jnp.int32)[None, :]).astype(f32)
    picked = jnp.dot(matched, window_row).reshape(9, frame_count)
    inside = (row_tile + row_step >= 0) & (row_tile + row_step < row_tiles)
    inside = inside & (col_tile + col_step >= 0) & (col_tile + col_step < col_tiles)
    slot_open = (picked > 0.5) & inside[:, None]
    slot_bias = jnp.where(slot_open, 0.0, -jnp.inf).astype(f32)
    key_bias = jnp.broadcast_to(
        slot_bias[:, :, None, None], (9, frame_count, tile_rows, tile_cols)
    ).reshape(-1)
    query_rows = query_in.reshape(-1, heads_dev, HEAD_DIM)
    saved_rows = saved_out.reshape(-1, heads_dev, HEAD_DIM)
    grad_rows = out_grad.reshape(-1, heads_dev, HEAD_DIM)
    key_rows = near_keys.reshape(-1, heads_dev, HEAD_DIM)
    value_rows = near_values.reshape(-1, heads_dev, HEAD_DIM)
    query_part, key_part, value_part = attend(
        query_rows, key_rows, value_rows, saved_rows, grad_rows, key_bias, score_scale
    )
    query_grad = query_part.reshape(frames_dev, 1, tile_rows, tile_cols, local_width)
    part_shape = (9, frame_count, tile_rows, tile_cols, local_width)
    key_block = key_part.reshape(part_shape)
    value_block = value_part.reshape(part_shape)
    key_sum = key_block[4].astype(f32)
    value_sum = value_block[4].astype(f32)
    for place_index, (row_move, col_move) in enumerate(neighbours):
        if (row_move, col_move) != (0, 0):
            offset = row_move * col_tiles + col_move
            if abs(offset) < plane_count:
                returned = passed_along(
                    (key_block[place_index], value_block[place_index]), "ha", offset
                )
                key_sum = key_sum + returned[0].astype(f32)
                value_sum = value_sum + returned[1].astype(f32)
    key_total, value_total = (
        lax.psum_scatter(key_sum, "ta", scatter_dimension=0, tiled=True),
        lax.psum_scatter(value_sum, "ta", scatter_dimension=0, tiled=True),
    )
    return (
        query_grad,
        key_total.astype(jnp.bfloat16)[:, None],
        value_total.astype(jnp.bfloat16)[:, None],
    )


def solution(mesh):
    return jax.shard_map(
        local,
        mesh=mesh,
        in_specs=(
            P("ta", "ha", None, None, "ga"),
            P("ta", "ha", None, None, "ga"),
            P("ta", "ha", None, None, "ga"),
            P("ta", "ha", None, None, "ga"),
            P("ta", "ha", None, None, "ga"),
            P(),
        ),
        out_specs=(
            P("ta", "ha", None, None, "ga"),
            P("ta", "ha", None, None, "ga"),
            P("ta", "ha", None, None, "ga"),
        ),
        check_vma=False,
    )
```

profile of v0, /device:TPU:9, one launch (start us, length us, event | category | flops | bytes accessed | tf_op | source)
XLA Modules:
  0.0 214.3 jit_solution(14967176099473543521)
XLA Ops:
  7.2 7.2 %all-gather = bf16[12,1,8,8,256]{4,3,2,1,0:T(8,128)(2,1)S(1)} all-gather(bf16[3,1,8,8,256]{4,3,2,1,0:T(8,128)(2,1)} %param.7), channel_id=2, replica_groups=mesh['ta'=4,'ha'=4,'ga'=2] {'ta'}, dimensions={0}, use_global_device_ids=true | all-gather | bytes 491520 | tf_op jit(solution)/shard_map/all_gather | solution.py:58
  15.1 3.2 %collective-permute-start.1 = (bf16[12,8,8,256]{3,2,1,0:T(8,128)(2,1)S(1)}, bf16[12,8,8,256]{3,2,1,0:T(8,128)(2,1)S(1)}, u32[]{:S(2)}, u32[]{:S(2)}) collective-permute-start(bf16[12,8,8,256]{3,2,1,0:T(8,128)(2,1)S(1)} %bitcast.84), channel_id=1, source_target_pairs={{0,2},{2,4},{4,6},{1,3},{3,5},{5,7},{8,10},{10,12},{12,14},{9,11},... | collective-permute-start | bytes 1179656 | tf_op jit(solution)/shard_map/ppermute | solution.py:13
  18.3 4.8 %collective-permute-start.2 = (bf16[12,8,8,256]{3,2,1,0:T(8,128)(2,1)S(1)}, bf16[12,8,8,256]{3,2,1,0:T(8,128)(2,1)S(1)}, u32[]{:S(2)}, u32[]{:S(2)}) collective-permute-start(bf16[12,8,8,256]{3,2,1,0:T(8,128)(2,1)S(1)} %bitcast.85), channel_id=1, source_target_pairs={{2,0},{4,2},{6,4},{3,1},{5,3},{7,5},{10,8},{12,10},{14,12},{11,9},... | collective-permute-start | bytes 1179656 | tf_op jit(solution)/shard_map/ppermute | solution.py:13
  23.8 8.1 %all-gather.1 = bf16[12,1,8,8,256]{4,3,2,1,0:T(8,128)(2,1)} all-gather(bf16[3,1,8,8,256]{4,3,2,1,0:T(8,128)(2,1)} %param.8), channel_id=3, replica_groups=mesh['ta'=4,'ha'=4,'ga'=2] {'ta'}, dimensions={0}, use_global_device_ids=true | all-gather | bytes 491520 | tf_op jit(solution)/shard_map/all_gather | solution.py:59
  43.0 7.2 %collective-permute-start.6 = (bf16[12,8,8,256]{3,2,1,0:T(8,128)(2,1)}, bf16[12,8,8,256]{3,2,1,0:T(8,128)(2,1)}, u32[]{:S(2)}, u32[]{:S(2)}) collective-permute-start(bf16[12,8,8,256]{3,2,1,0:T(8,128)(2,1)} %bitcast.13), channel_id=1, source_target_pairs={{2,0},{4,2},{6,4},{3,1},{5,3},{7,5},{10,8},{12,10},{14,12},{11,9},... | collective-permute-start | bytes 1179656 | tf_op jit(solution)/shard_map/ppermute | solution.py:13
  55.8 6.5 %reshape.138 = bf16[6912,2,128]{2,1,0:T(2,128)(2,1)S(1)} reshape(bf16[9,12,8,8,256]{4,3,2,1,0:T(8,128)(2,1)} %broadcast_dynamic-update-slice_fusion.3) | data formatting | bytes 7077888 | tf_op jit(solution)/shard_map/reshape | solution.py:99
  62.3 2.5 %multiply_add_fusion = f32[2,6912,192]{1,2,0:T(8,128)S(1)} fusion(f32[6912]{0:T(1024)} %add.145, bf16[6912,2,128]{2,1,0:T(2,128)(2,1)S(1)} %reshape.138, bf16[192,2,128]{2,1,0:T(2,128)(2,1)} %reshape.139), kind=kOutput, calls=%fused_computation.7 | convolution fusion | flops 684785664 | bytes 14281728 | tf_op jit(solution)/shard_map/qhd,khd->hqk/dot_general | solution.py:19
  64.8 5.9 %fusion.43 = (f32[2,192]{1,0:T(2,128)S(1)}, f32[2,192,6912]{2,1,0:T(8,128)}) fusion(f32[2,6912,192]{1,2,0:T(8,128)S(1)} %multiply_add_fusion), kind=kOutput, calls=%fused_computation.77 | output fusion | flops 5315327 | bytes 21235200 | tf_op jit(solution)/shard_map/sub | solution.py:23
  70.7 6.9 %fusion.9 = bf16[6912,2,128]{2,0,1:T(8,128)(2,1)S(1)} fusion(f32[2,192,6912]{2,1,0:T(8,128)} %get-tuple-element.20, f32[2,192]{1,0:T(2,128)S(1)} %get-tuple-element.19, bf16[192,2,128]{2,1,0:T(2,128)(2,1)S(1)} %copy-done.4), kind=kOutput, calls=%fused_computation.12 | convolution fusion | flops 686555136 | bytes 14255616 | tf_op jit(solution)/shard_map/hqk,qhd->khd/dot_general | solution.py:26
  99.8 3.4 %collective-permute-start.14 = (bf16[12,8,8,256]{3,2,1,0:T(8,128)(2,1)}, bf16[12,8,8,256]{3,2,1,0:T(8,128)(2,1)}, u32[]{:S(2)}, u32[]{:S(2)}) collective-permute-start(bf16[12,8,8,256]{3,2,1,0:T(8,128)(2,1)} %squeeze.40), channel_id=1, source_target_pairs={{0,2},{2,4},{4,6},{1,3},{3,5},{5,7},{8,10},{10,12},{12,14},{9,11},... | collective-permute-start | bytes 1179656 | tf_op jit(solution)/shard_map/ppermute | solution.py:13
  111.4 2.7 %reshape.145 = f32[12,8,8,256]{3,2,1,0:T(8,128)} reshape(f32[768,2,128]{2,1,0:T(2,128)} %copy.47) | data formatting | bytes 1572864 | tf_op jit(solution)/shard_map/convert_element_type | solution.py:109
  116.9 7.8 %reshape.140 = bf16[6912,2,128]{2,1,0:T(2,128)(2,1)} reshape(bf16[9,12,8,8,256]{4,3,2,1,0:T(8,128)(2,1)} %broadcast_dynamic-update-slice_fusion.2) | data formatting | bytes 7077888 | tf_op jit(solution)/shard_map/reshape | solution.py:100
  124.7 2.8 %convert_add_fusion = f32[12,8,8,256]{3,2,1,0:T(8,128)} fusion(bf16[12,8,8,256]{3,2,1,0:T(8,128)(2,1)} %collective-permute-done.15, bf16[12,8,8,256]{3,2,1,0:T(8,128)(2,1)} %collective-permute-done.14, bf16[12,8,8,256]{3,2,1,0:T(8,128)(2,1)} %collective-permute-done.13, f32[12,8,8,256]{3,2,1,0:T(8,128)} %reshape.145, ...), kind=kLoop, calls=%fused_computation.21 | loop fusion | flops 1572864 | bytes 3145728 | tf_op jit(solution)/shard_map/add | solution.py:118
  127.6 7.6 %fusion.3 = bf16[2,192,6912]{2,1,0:T(8,128)(2,1)S(1)} fusion(f32[2,192]{1,0:T(2,128)S(1)} %copy.62, f32[2,192,6912]{2,1,0:T(8,128)} %get-tuple-element.20, f32[2,192]{1,0:T(2,128)S(1)} %get-tuple-element.19, bf16[6912,2,128]{2,1,0:T(2,128)(2,1)} %reshape.140, bf16[192,2,128]{2,1,0:T(2,128)(2,1)} %copy-done.3), kind=kOutput, calls=%fused_computation.4 | convolution fusion | flops 692748288 | bytes 19565568 | tf_op jit(solution)/shard_map/qhd,khd->hqk/dot_general | solution.py:29
  135.2 2.9 %fusion.8 = bf16[6912,2,128]{2,0,1:T(8,128)(2,1)S(1)} fusion(bf16[2,192,6912]{2,1,0:T(8,128)(2,1)S(1)} %fusion.3, bf16[192,2,128]{2,1,0:T(2,128)(2,1)S(1)} %copy-done.2), kind=kOutput, calls=%fused_computation.11 | convolution fusion | flops 681246720 | bytes 8945664 | tf_op jit(solution)/shard_map/hqk,qhd->khd/dot_general | solution.py:35
  142.6 4.4 %collective-permute-start.10 = (bf16[12,8,8,256]{3,2,1,0:T(8,128)(2,1)}, bf16[12,8,8,256]{3,2,1,0:T(8,128)(2,1)}, u32[]{:S(2)}, u32[]{:S(2)}) collective-permute-start(bf16[12,8,8,256]{3,2,1,0:T(8,128)(2,1)} %squeeze.36), channel_id=1, source_target_pairs={{0,2},{2,4},{4,6},{1,3},{3,5},{5,7},{8,10},{10,12},{12,14},{9,11},... | collective-permute-start | bytes 1179656 | tf_op jit(solution)/shard_map/ppermute | solution.py:13
  147.0 2.2 %copy.45 = bf16[768,2,128]{2,1,0:T(2,128)(2,1)} copy(bf16[768,2,128]{2,0,1:T(8,128)(2,1)} %get-tuple-element.15) | data formatting | bytes 786432 | tf_op jit(solution)/shard_map/slice | solution.py:115
  162.4 4.0 %collective-permute-start.9 = (bf16[12,8,8,256]{3,2,1,0:T(8,128)(2,1)}, bf16[12,8,8,256]{3,2,1,0:T(8,128)(2,1)}, u32[]{:S(2)}, u32[]{:S(2)}) collective-permute-start(bf16[12,8,8,256]{3,2,1,0:T(8,128)(2,1)} %squeeze.35), channel_id=1, source_target_pairs={{2,0},{4,2},{6,4},{3,1},{5,3},{7,5},{10,8},{12,10},{14,12},{11,9},... | collective-permute-start | bytes 1179656 | tf_op jit(solution)/shard_map/ppermute | solution.py:13
  166.3 2.6 %copy.41 = f32[768,2,128]{2,1,0:T(2,128)} copy(f32[768,2,128]{2,0,1:T(8,128)} %get-tuple-element.18) | data formatting | bytes 1572864 | tf_op jit(solution)/shard_map/convert_element_type | solution.py:108
  169.0 2.7 %reshape.144 = f32[12,8,8,256]{3,2,1,0:T(8,128)} reshape(f32[768,2,128]{2,1,0:T(2,128)} %copy.41) | data formatting | bytes 1572864 | tf_op jit(solution)/shard_map/convert_element_type | solution.py:108
  171.6 9.6 %collective-permute-done.9 = bf16[12,8,8,256]{3,2,1,0:T(8,128)(2,1)} collective-permute-done((bf16[12,8,8,256]{3,2,1,0:T(8,128)(2,1)}, bf16[12,8,8,256]{3,2,1,0:T(8,128)(2,1)}, u32[]{:S(2)}, u32[]{:S(2)}) %collective-permute-start.9) | collective-permute-done | bytes 393248 | tf_op jit(solution)/shard_map/ppermute | solution.py:13
  181.3 2.8 %convert_add_fusion.1 = f32[12,8,8,256]{3,2,1,0:T(8,128)} fusion(bf16[12,8,8,256]{3,2,1,0:T(8,128)(2,1)} %collective-permute-done.11, bf16[12,8,8,256]{3,2,1,0:T(8,128)(2,1)} %collective-permute-done.10, bf16[12,8,8,256]{3,2,1,0:T(8,128)(2,1)} %collective-permute-done.9, f32[12,8,8,256]{3,2,1,0:T(8,128)} %reshape.144, ...), kind=kLoop, calls=%fused_computation.22 | loop fusion | flops 1572864 | bytes 3145728 | tf_op jit(solution)/shard_map/add | solution.py:117
  184.1 4.0 %fusion.18 = bf16[192,2,128]{2,0,1:T(8,128)(2,1)S(1)} fusion(bf16[2,192,6912]{2,1,0:T(8,128)(2,1)} %copy-done, bf16[6912,2,128]{2,1,0:T(2,128)(2,1)S(1)} %reshape.138), kind=kOutput, calls=%fused_computation.20 | convolution fusion | flops 679526400 | bytes 8945664 | tf_op jit(solution)/shard_map/hqk,khd->qhd/dot_general | solution.py:32
  190.5 15.3 %reduce-scatter.3.cloned.1.call-done = f32[3,8,8,256]{3,2,1,0:T(8,128)} async-done(((f32[12,8,8,256]{3,2,1,0:T(8,128)}), f32[3,8,8,256]{3,2,1,0:T(8,128)}) %reduce-scatter.3.cloned.1.call-update) | async-done | bytes 196624 | tf_op jit(solution)/shard_map/reduce_scatter | solution.py:120
  (90 shorter events, 72.9 us)
Async XLA Ops:
  7.2 31.4 %copy-start.5 = (bf16[3,1,8,8,256]{4,3,2,1,0:T(8,128)(2,1)S(1)}, bf16[3,1,8,8,256]{4,3,2,1,0:T(8,128)(2,1)}, u32[]{:S(2)}) copy-start(bf16[3,1,8,8,256]{4,3,2,1,0:T(8,128)(2,1)} %param.6) | copy-start | bytes 294916
  7.2 181.8 %reduce-scatter.5.cloned.1.call-start = ((), (), s32[]{:S(2)}) async-start(), calls=%async_computation.3 | async-start | bytes 983040 | tf_op jit(solution)/shard_map/reduce_scatter | solution.py:121
  14.4 25.9 %collective-permute-start = (bf16[12,8,8,256]{3,2,1,0:T(8,128)(2,1)S(1)}, bf16[12,8,8,256]{3,2,1,0:T(8,128)(2,1)S(1)}, u32[]{:S(2)}, u32[]{:S(2)}) collective-permute-start(bf16[12,8,8,256]{3,2,1,0:T(8,128)(2,1)S(1)} %bitcast.83), channel_id=1, source_target_pairs={{0,6},{1,7},{8,14},{9,15},{16,22},{17,23},{24,30},{25,31}} | collective-permute-start | bytes 1179656 | tf_op jit(solution)/shard_map/ppermute | solution.py:13
  15.1 28.0 %collective-permute-start.1 = (bf16[12,8,8,256]{3,2,1,0:T(8,128)(2,1)S(1)}, bf16[12,8,8,256]{3,2,1,0:T(8,128)(2,1)S(1)}, u32[]{:S(2)}, u32[]{:S(2)}) collective-permute-start(bf16[12,8,8,256]{3,2,1,0:T(8,128)(2,1)S(1)} %bitcast.84), channel_id=1, source_target_pairs={{0,2},{2,4},{4,6},{1,3},{3,5},{5,7},{8,10},{10,12},{12,14},{9,11},... | collective-permute-start | bytes 1179656 | tf_op jit(solution)/shard_map/ppermute | solution.py:13
  18.3 33.5 %collective-permute-start.2 = (bf16[12,8,8,256]{3,2,1,0:T(8,128)(2,1)S(1)}, bf16[12,8,8,256]{3,2,1,0:T(8,128)(2,1)S(1)}, u32[]{:S(2)}, u32[]{:S(2)}) collective-permute-start(bf16[12,8,8,256]{3,2,1,0:T(8,128)(2,1)S(1)} %bitcast.85), channel_id=1, source_target_pairs={{2,0},{4,2},{6,4},{3,1},{5,3},{7,5},{10,8},{12,10},{14,12},{11,9},... | collective-permute-start | bytes 1179656 | tf_op jit(solution)/shard_map/ppermute | solution.py:13
  23.1 30.9 %collective-permute-start.3 = (bf16[12,8,8,256]{3,2,1,0:T(8,128)(2,1)S(1)}, bf16[12,8,8,256]{3,2,1,0:T(8,128)(2,1)S(1)}, u32[]{:S(2)}, u32[]{:S(2)}) collective-permute-start(bf16[12,8,8,256]{3,2,1,0:T(8,128)(2,1)S(1)} %bitcast.86), channel_id=1, source_target_pairs={{6,0},{7,1},{14,8},{15,9},{22,16},{23,17},{30,24},{31,25}} | collective-permute-start | bytes 1179656 | tf_op jit(solution)/shard_map/ppermute | solution.py:13
  31.9 64.1 %collective-permute-start.4 = (bf16[12,8,8,256]{3,2,1,0:T(8,128)(2,1)}, bf16[12,8,8,256]{3,2,1,0:T(8,128)(2,1)}, u32[]{:S(2)}, u32[]{:S(2)}) collective-permute-start(bf16[12,8,8,256]{3,2,1,0:T(8,128)(2,1)} %bitcast.13), channel_id=1, source_target_pairs={{0,6},{1,7},{8,14},{9,15},{16,22},{17,23},{24,30},{25,31}} | collective-permute-start | bytes 1179656 | tf_op jit(solution)/shard_map/ppermute | solution.py:13
  34.3 2.3 %copy-start.3 = (bf16[192,2,128]{2,1,0:T(2,128)(2,1)}, bf16[192,2,128]{2,1,0:T(2,128)(2,1)S(1)}, u32[]{:S(2)}) copy-start(bf16[192,2,128]{2,1,0:T(2,128)(2,1)S(1)} %reshape.141) | copy-start | bytes 294916
  40.3 59.5 %collective-permute-start.5 = (bf16[12,8,8,256]{3,2,1,0:T(8,128)(2,1)}, bf16[12,8,8,256]{3,2,1,0:T(8,128)(2,1)}, u32[]{:S(2)}, u32[]{:S(2)}) collective-permute-start(bf16[12,8,8,256]{3,2,1,0:T(8,128)(2,1)} %bitcast.13), channel_id=1, source_target_pairs={{0,2},{2,4},{4,6},{1,3},{3,5},{5,7},{8,10},{10,12},{12,14},{9,11},... | collective-permute-start | bytes 1179656 | tf_op jit(solution)/shard_map/ppermute | solution.py:13
  43.0 63.7 %collective-permute-start.6 = (bf16[12,8,8,256]{3,2,1,0:T(8,128)(2,1)}, bf16[12,8,8,256]{3,2,1,0:T(8,128)(2,1)}, u32[]{:S(2)}, u32[]{:S(2)}) collective-permute-start(bf16[12,8,8,256]{3,2,1,0:T(8,128)(2,1)} %bitcast.13), channel_id=1, source_target_pairs={{2,0},{4,2},{6,4},{3,1},{5,3},{7,5},{10,8},{12,10},{14,12},{11,9},... | collective-permute-start | bytes 1179656 | tf_op jit(solution)/shard_map/ppermute | solution.py:13
  51.8 62.3 %collective-permute-start.7 = (bf16[12,8,8,256]{3,2,1,0:T(8,128)(2,1)}, bf16[12,8,8,256]{3,2,1,0:T(8,128)(2,1)}, u32[]{:S(2)}, u32[]{:S(2)}) collective-permute-start(bf16[12,8,8,256]{3,2,1,0:T(8,128)(2,1)} %bitcast.13), channel_id=1, source_target_pairs={{6,0},{7,1},{14,8},{15,9},{22,16},{23,17},{30,24},{31,25}} | collective-permute-start | bytes 1179656 | tf_op jit(solution)/shard_map/ppermute | solution.py:13
  64.7 5.9 %copy-start.4 = (bf16[192,2,128]{2,1,0:T(2,128)(2,1)S(1)}, bf16[192,2,128]{2,1,0:T(2,128)(2,1)}, u32[]{:S(2)}) copy-start(bf16[192,2,128]{2,1,0:T(2,128)(2,1)} %copy-done.3) | copy-start | bytes 294916
  82.1 42.6 %collective-permute-start.12 = (bf16[12,8,8,256]{3,2,1,0:T(8,128)(2,1)}, bf16[12,8,8,256]{3,2,1,0:T(8,128)(2,1)}, u32[]{:S(2)}, u32[]{:S(2)}) collective-permute-start(bf16[12,8,8,256]{3,2,1,0:T(8,128)(2,1)} %squeeze.38), channel_id=1, source_target_pairs={{6,0},{7,1},{14,8},{15,9},{22,16},{23,17},{30,24},{31,25}} | collective-permute-start | bytes 1179656 | tf_op jit(solution)/shard_map/ppermute | solution.py:13
  96.0 13.9 %copy-start.1 = (f32[768,2,128]{2,0,1:T(8,128)S(1)}, f32[768,2,128]{2,0,1:T(8,128)}, u32[]{:S(2)}) copy-start(f32[768,2,128]{2,0,1:T(8,128)} %get-tuple-element.13) | copy-start | bytes 2359300
  96.0 28.7 %collective-permute-start.13 = (bf16[12,8,8,256]{3,2,1,0:T(8,128)(2,1)}, bf16[12,8,8,256]{3,2,1,0:T(8,128)(2,1)}, u32[]{:S(2)}, u32[]{:S(2)}) collective-permute-start(bf16[12,8,8,256]{3,2,1,0:T(8,128)(2,1)} %squeeze.39), channel_id=1, source_target_pairs={{2,0},{4,2},{6,4},{3,1},{5,3},{7,5},{10,8},{12,10},{14,12},{11,9},... | collective-permute-start | bytes 1179656 | tf_op jit(solution)/shard_map/ppermute | solution.py:13
  99.8 24.9 %collective-permute-start.14 = (bf16[12,8,8,256]{3,2,1,0:T(8,128)(2,1)}, bf16[12,8,8,256]{3,2,1,0:T(8,128)(2,1)}, u32[]{:S(2)}, u32[]{:S(2)}) collective-permute-start(bf16[12,8,8,256]{3,2,1,0:T(8,128)(2,1)} %squeeze.40), channel_id=1, source_target_pairs={{0,2},{2,4},{4,6},{1,3},{3,5},{5,7},{8,10},{10,12},{12,14},{9,11},... | collective-permute-start | bytes 1179656 | tf_op jit(solution)/shard_map/ppermute | solution.py:13
  106.7 18.0 %collective-permute-start.15 = (bf16[12,8,8,256]{3,2,1,0:T(8,128)(2,1)}, bf16[12,8,8,256]{3,2,1,0:T(8,128)(2,1)}, u32[]{:S(2)}, u32[]{:S(2)}) collective-permute-start(bf16[12,8,8,256]{3,2,1,0:T(8,128)(2,1)} %squeeze.41), channel_id=1, source_target_pairs={{0,6},{1,7},{8,14},{9,15},{16,22},{17,23},{24,30},{25,31}} | collective-permute-start | bytes 1179656 | tf_op jit(solution)/shard_map/ppermute | solution.py:13
  127.5 78.3 %reduce-scatter.3.cloned.1.call-start = ((), (), s32[]{:S(2)}) async-start(), calls=%async_computation.2 | async-start | bytes 983040 | tf_op jit(solution)/shard_map/reduce_scatter | solution.py:120
  127.6 7.7 %copy-start.2 = (bf16[192,2,128]{2,1,0:T(2,128)(2,1)S(1)}, bf16[192,2,128]{2,1,0:T(2,128)(2,1)}, u32[]{:S(2)}) copy-start(bf16[192,2,128]{2,1,0:T(2,128)(2,1)} %reshape.139) | copy-start | bytes 294916
  135.2 2.9 %copy-start = (bf16[2,192,6912]{2,1,0:T(8,128)(2,1)}, bf16[2,192,6912]{2,1,0:T(8,128)(2,1)S(1)}, u32[]{:S(2)}) copy-start(bf16[2,192,6912]{2,1,0:T(8,128)(2,1)S(1)} %fusion.3) | copy-start | bytes 15925252
  142.6 29.0 %collective-permute-start.10 = (bf16[12,8,8,256]{3,2,1,0:T(8,128)(2,1)}, bf16[12,8,8,256]{3,2,1,0:T(8,128)(2,1)}, u32[]{:S(2)}, u32[]{:S(2)}) collective-permute-start(bf16[12,8,8,256]{3,2,1,0:T(8,128)(2,1)} %squeeze.36), channel_id=1, source_target_pairs={{0,2},{2,4},{4,6},{1,3},{3,5},{5,7},{8,10},{10,12},{12,14},{9,11},... | collective-permute-start | bytes 1179656 | tf_op jit(solution)/shard_map/ppermute | solution.py:13
  151.2 20.4 %collective-permute-start.11 = (bf16[12,8,8,256]{3,2,1,0:T(8,128)(2,1)}, bf16[12,8,8,256]{3,2,1,0:T(8,128)(2,1)}, u32[]{:S(2)}, u32[]{:S(2)}) collective-permute-start(bf16[12,8,8,256]{3,2,1,0:T(8,128)(2,1)} %squeeze.37), channel_id=1, source_target_pairs={{0,6},{1,7},{8,14},{9,15},{16,22},{17,23},{24,30},{25,31}} | collective-permute-start | bytes 1179656 | tf_op jit(solution)/shard_map/ppermute | solution.py:13
  156.8 14.8 %collective-permute-start.8 = (bf16[12,8,8,256]{3,2,1,0:T(8,128)(2,1)}, bf16[12,8,8,256]{3,2,1,0:T(8,128)(2,1)}, u32[]{:S(2)}, u32[]{:S(2)}) collective-permute-start(bf16[12,8,8,256]{3,2,1,0:T(8,128)(2,1)} %squeeze.34), channel_id=1, source_target_pairs={{6,0},{7,1},{14,8},{15,9},{22,16},{23,17},{30,24},{31,25}} | collective-permute-start | bytes 1179656 | tf_op jit(solution)/shard_map/ppermute | solution.py:13
  162.4 18.9 %collective-permute-start.9 = (bf16[12,8,8,256]{3,2,1,0:T(8,128)(2,1)}, bf16[12,8,8,256]{3,2,1,0:T(8,128)(2,1)}, u32[]{:S(2)}, u32[]{:S(2)}) collective-permute-start(bf16[12,8,8,256]{3,2,1,0:T(8,128)(2,1)} %squeeze.35), channel_id=1, source_target_pairs={{2,0},{4,2},{6,4},{3,1},{5,3},{7,5},{10,8},{12,10},{14,12},{11,9},... | collective-permute-start | bytes 1179656 | tf_op jit(solution)/shard_map/ppermute | solution.py:13
Sparse Core Ops, SparseCore 0:
  127.6 24.6 reduce-scatter.4
  184.2 21.6 reduce-scatter.2
where the time goes:
time: 218 us; the launch traced here: 214 us
  local copies, waits for them, and re-layouts  76.3 us (35%)
  starting transfers between devices  40.7 us (19%)
  waiting for transfers between devices  25 us (11%)
  matrix products  24.9 us (11%)
  other arithmetic  17.7 us (8%)
  blocking collectives  15.3 us (7%)
  between operations  14.3 us (7%)
    ppermute x16, starting transfers between devices, passed_along(): return lax.ppermute(block, axis, route)  40.6 us
    reduce_scatter x1, waiting for transfers between devices, local(): lax.psum_scatter(key_sum, 'ta', scatter_dimension=0, tiled=True)  15.3 us
    unnamed x24, local copies, waits for them, and re-layouts  14.8 us
    ppermute x16, waiting for transfers between devices, passed_along(): return lax.ppermute(block, axis, route)  9.68 us
    all_gather x1, blocking collectives, local(): lax.all_gather(own_pair[1], 'ta', axis=0, tiled=True)  8.14 us
    squeeze x4, local copies, waits for them, and re-layouts, local(): key_block[place_index]  8.01 us
    squeeze x4, local copies, waits for them, and re-layouts, local(): value_block[place_index]  7.98 us
    reshape x1, local copies, waits for them, and re-layouts, local(): value_rows = near_values.reshape(-1, heads_dev, HEAD_DIM)  7.82 us
  transfers between devices with their start and end apart: 18, of which 2 were waited for; matrix products, arithmetic and copies ran while one was open for 53% of the time, Pallas kernels for 0%

commit v1 on v0

v1 whole, which is shorter than its diff:
```python
import functools

import jax
import jax.numpy as jnp
from jax import lax
from jax.experimental import pallas as pl
from jax.experimental.pallas import tpu as pltpu
from jax.sharding import PartitionSpec as P

HEAD_DIM = 128
TILE_T = 6
LOG2_E = 1.4426950408889634
LOWEST = -1e30
MESH = pl.DeviceIdType.MESH
KEY, QUERY, GRAD, VALUE = range(4)


def kernel(
    dims,
    mask_ref,
    q_ref,
    k_ref,
    v_ref,
    o_ref,
    g_ref,
    dq_ref,
    dk_ref,
    dv_ref,
    near,
    stats,
    raised,
    lifted_own,
    dq_acc,
    dk_acc,
    dv_acc,
    pair_sem,
    plane_sem,
    span_sem,
    recv_sem,
    stat_send,
    stat_recv,
):
    f32, bf16 = jnp.float32, jnp.bfloat16
    n_ta, row_tiles, col_tiles, frames_dev, heads, moves = dims
    rows = q_ref.shape[0]
    n_slot = len(moves)
    centre = moves.index((0, 0))
    others = [s for s in range(n_slot) if s != centre]
    order = [centre] + others
    keys = n_ta * rows
    scale = HEAD_DIM ** (-0.5)
    to_two = scale * LOG2_E
    n_low = 2 if n_ta % 2 == 0 else 1
    n_high = n_ta // n_low

    time = lax.axis_index("ta")
    plane = lax.axis_index("ha")
    group = lax.axis_index("ga")
    high, low = time // n_low, time % n_low
    row_tile = plane // col_tiles
    col_tile = plane % col_tiles
    inside = [
        (row_tile + dr >= 0)
        & (row_tile + dr < row_tiles)
        & (col_tile + dc >= 0)
        & (col_tile + dc < col_tiles)
        for dr, dc in moves
    ]
    own = {KEY: k_ref, QUERY: q_ref, GRAD: g_ref, VALUE: v_ref}

    def shifted(s):
        dr, dc = moves[s]
        return plane + dr * col_tiles + dc

    def back(s):
        return n_slot - 1 - s

    def if_inside(s, do):
        if s == centre:
            do()
        else:
            pl.when(inside[s])(do)

    def push(src, a, s, j, send_sem, device):
        return pltpu.make_async_remote_copy(
            src_ref=src,
            dst_ref=near.at[a, s, j],
            send_sem=send_sem,
            recv_sem=recv_sem.at[a, s, j],
            device_id=device,
            device_id_type=MESH,
        )

    def held(a, s, d):
        if s == centre and d == 0:
            return own[a], time
        j = (high + d) % n_high * n_low + low
        return near.at[a, s, j], j

    def span_copy(a, d):
        j = (high + d) % n_high * n_low + low
        return push(own[a], a, centre, time, span_sem.at[a, d], (j, plane, group))

    def plane_copy(a, s, d):
        src, j = held(a, centre, d)
        return push(src, a, back(s), j, plane_sem.at[a, s, d], (time, shifted(s), group))

    def pair_copy(a, s, d):
        src, j = held(a, s, d)
        partner = high * n_low + 1 - low
        return push(src, a, s, j, pair_sem.at[a, s, d], (partner, plane, group))

    def arrived(a, s, j):
        block = near.at[a, s, j]
        push(block, a, s, j, recv_sem.at[a, s, j], (time, plane, group)).wait_recv()

    def wait_chain(a, s):
        for d in range(n_high):
            if s != centre or d != 0:
                arrived(a, s, (high + d) % n_high * n_low + low)

    def wait_pair(a, s):
        if n_low == 2:
            for h in range(n_high):
                arrived(a, s, h * n_low + 1 - low)

    def start_pair(a, s, d):
        if n_low == 2:
            pair_copy(a, s, d).start()

    def start_planes(a, d):
        for s in others:
            if_inside(s, lambda s=s: plane_copy(a, s, d).start())

    def pass_on_span(a):
        wait_chain(a, centre)
        for d in range(1, n_high):
            start_planes(a, d)
            start_pair(a, centre, d)

    def pass_on_planes(a):
        for s in others:

            def do(s=s):
                wait_chain(a, s)
                for d in range(n_high):
                    start_pair(a, s, d)

            if_inside(s, do)

    def wait_rest(a, s):
        if_inside(s, lambda: wait_pair(a, s))

    def stat_copy(s, j):
        return pltpu.make_async_remote_copy(
            src_ref=stats.at[centre, time],
            dst_ref=stats.at[back(s), time],
            send_sem=stat_send.at[s, j],
            recv_sem=stat_recv.at[back(s), time],
            device_id=(j, shifted(s), group),
            device_id_type=MESH,
        )

    def stat_arrived(s, j):
        block = stats.at[s, j]
        pltpu.make_async_remote_copy(
            src_ref=block,
            dst_ref=block,
            send_sem=stat_send.at[s, j],
            recv_sem=stat_recv.at[s, j],
            device_id=(time, plane, group),
            device_id_type=MESH,
        ).wait_recv()

    def each_peer(s, do):
        for j in range(n_ta):
            if s == centre:
                pl.when(time != j)(functools.partial(do, s, j))
            else:
                pl.when(inside[s])(functools.partial(do, s, j))

    barrier = pltpu.get_barrier_semaphore()

    def greet(s, j):
        pl.semaphore_signal(
            barrier, inc=1, device_id=(j, shifted(s), group), device_id_type=MESH
        )

    for s in order:
        each_peer(s, greet)
    planes = sum(jnp.where(inside[s], 1, 0) for s in range(n_slot))
    pl.semaphore_wait(barrier, planes * n_ta - 1)

    for a in (KEY, QUERY, GRAD, VALUE):
        for d in range(1, n_high):
            span_copy(a, d).start()
        if a == KEY:
            start_planes(a, 0)
    for a in (KEY, QUERY, GRAD, VALUE):
        start_pair(a, centre, 0)

    for a in (KEY, QUERY, GRAD, VALUE):
        near[a, centre, time] = own[a][...]
    for s in others:

        @pl.when(jnp.logical_not(inside[s]))
        def _(s=s):
            for a in (KEY, QUERY, GRAD, VALUE):
                near[a, s] = jnp.zeros(near.shape[2:], bf16)
            stats[s] = jnp.zeros(stats.shape[1:], f32)

    head_of = [slice(h * HEAD_DIM, (h + 1) * HEAD_DIM) for h in range(heads)]
    column = lax.broadcasted_iota(jnp.int32, (1, keys), 1)
    row_dot = [
        jnp.sum(
            g_ref[:, head_of[h]].astype(f32) * o_ref[:, head_of[h]].astype(f32),
            axis=-1,
            keepdims=True,
        )
        * scale
        for h in range(heads)
    ]

    def tile_time(j):
        return j * frames_dev // TILE_T

    def open_bias(s, as_query):
        dr, dc = moves[s]
        bias = jnp.full((1, keys), -jnp.inf, f32)
        for j in range(n_ta):
            if as_query:
                query_time, time_step = tile_time(time), tile_time(j) - tile_time(time)
                query_row, query_col, row_step, col_step = row_tile, col_tile, dr, dc
            else:
                query_time, time_step = tile_time(j), tile_time(time) - tile_time(j)
                query_row = jnp.clip(row_tile + dr, 0, row_tiles - 1)
                query_col = jnp.clip(col_tile + dc, 0, col_tiles - 1)
                row_step, col_step = -dr, -dc
            close = (time_step >= -1) & (time_step <= 1)
            code = (jnp.clip(time_step, -1, 1) + 1) * 9 + (row_step + 1) * 3 + (col_step + 1)
            tile = (query_time * row_tiles + query_row) * col_tiles + query_col
            is_open = (mask_ref[tile * 27 + code] == 1) & close & inside[s]
            here = (column >= j * rows) & (column < (j + 1) * rows)
            bias = jnp.where(here & is_open, 0.0, bias)
        return bias

    def dot(a, b, dims):
        return lax.dot_general(a, b, (dims, ((), ())), preferred_element_type=f32)

    def block_of(a, s, h):
        return near[a, s, :, :, head_of[h]].reshape(keys, HEAD_DIM)

    slot_max = {}
    slot_sum = {}

    def own_scores(s):
        bias = open_bias(s, True)
        for h in range(heads):
            scores = dot(q_ref[:, head_of[h]], block_of(KEY, s, h), ((1,), (1,))) + bias
            top = jnp.maximum(jnp.max(scores, axis=-1, keepdims=True), LOWEST)
            lifted = jnp.exp2((scores - top) * to_two)
            raised[s, h] = lifted
            slot_max[s, h] = top
            slot_sum[s, h] = jnp.sum(lifted, axis=-1, keepdims=True)

    pass_on_span(KEY)
    start_planes(QUERY, 0)
    wait_rest(KEY, centre)
    own_scores(centre)
    pass_on_span(QUERY)
    pass_on_planes(KEY)
    start_planes(GRAD, 0)
    for s in others:
        wait_rest(KEY, s)
        own_scores(s)
    pass_on_span(GRAD)
    start_planes(VALUE, 0)

    factor = {}
    columns = []
    for h in range(heads):
        top = slot_max[centre, h]
        for s in others:
            top = jnp.maximum(top, slot_max[s, h])
        gain = {s: jnp.exp2((slot_max[s, h] - top) * to_two) for s in order}
        total = gain[centre] * slot_sum[centre, h]
        for s in others:
            total = total + gain[s] * slot_sum[s, h]
        for s in order:
            factor[s, h] = gain[s] / total
        columns.append(top * to_two + jnp.log2(total))
    columns = columns + row_dot
    lane = lax.broadcasted_iota(jnp.int32, (rows, HEAD_DIM), 1)
    table = jnp.zeros((rows, HEAD_DIM), f32)
    for index, col in enumerate(columns):
        table = jnp.where(lane == index, col, table)
    stats[centre, time] = table.T[: stats.shape[2]]
    for s in order:
        each_peer(s, lambda s, j: stat_copy(s, j).start())
    pass_on_span(VALUE)

    def stat_rows(s):
        return jnp.concatenate([stats[s, j] for j in range(n_ta)], axis=1)

    def key_weights(s):
        each_peer(s, stat_arrived)
        bias = open_bias(s, False)
        table = stat_rows(s)
        for h in range(heads):
            scores = dot(k_ref[:, head_of[h]], block_of(QUERY, s, h), ((1,), (1,)))
            lifted_own[s, h] = jnp.exp2(scores * to_two + (bias - table[h : h + 1]))

    def add(acc, h, first, part):
        if first:
            acc[:, head_of[h]] = part
        else:
            acc[:, head_of[h]] += part

    def key_grads(s):
        table = stat_rows(s)
        for h in range(heads):
            grads = block_of(GRAD, s, h)
            weights = lifted_own[s, h]
            add(dv_acc, h, s == centre, dot(weights.astype(bf16), grads, ((1,), (0,))))
            weight_grad = dot(v_ref[:, head_of[h]], grads, ((1,), (1,)))
            shift = table[heads + h : heads + h + 1]
            score_grad = (weights * (weight_grad * scale - shift)).astype(bf16)
            part = dot(score_grad, block_of(QUERY, s, h), ((1,), (0,)))
            add(dk_acc, h, s == centre, part)

    def query_grads(s):
        for h in range(heads):
            weight_grad = dot(g_ref[:, head_of[h]], block_of(VALUE, s, h), ((1,), (1,)))
            weights = raised[s, h] * factor[s, h]
            score_grad = (weights * (weight_grad * scale - row_dot[h])).astype(bf16)
            part = dot(score_grad, block_of(KEY, s, h), ((1,), (0,)))
            add(dq_acc, h, s == centre, part)

    pass_on_planes(QUERY)
    for s in order:
        wait_rest(QUERY, s)
        key_weights(s)
    wait_rest(GRAD, centre)
    key_grads(centre)
    wait_rest(VALUE, centre)
    query_grads(centre)
    pass_on_planes(GRAD)
    for s in others:
        wait_rest(GRAD, s)
        key_grads(s)
    pass_on_planes(VALUE)
    dk_ref[...] = dk_acc[...].astype(bf16)
    dv_ref[...] = dv_acc[...].astype(bf16)
    for s in others:
        wait_rest(VALUE, s)
        query_grads(s)
    dq_ref[...] = dq_acc[...].astype(bf16)

    for a in (KEY, QUERY, GRAD, VALUE):
        for d in range(1, n_high):
            span_copy(a, d).wait_send()
        for s in order:

            def finish(s=s, a=a):
                for d in range(n_high):
                    if s != centre:
                        plane_copy(a, s, d).wait_send()
                    if n_low == 2:
                        pair_copy(a, s, d).wait_send()

            if_inside(s, finish)
    for s in order:
        each_peer(s, lambda s, j: stat_copy(s, j).wait_send())


def local(n_ta, query_in, key_in, value_in, saved_out, out_grad, window_mask):
    f32, bf16 = jnp.float32, jnp.bfloat16
    shape = query_in.shape
    frames_dev, _, tile_rows, tile_cols, width = shape
    rows = frames_dev * tile_rows * tile_cols
    heads = width // HEAD_DIM
    _, row_tiles, col_tiles, _ = window_mask.shape
    moves = [
        (dr, dc)
        for dr in (-1, 0, 1)
        for dc in (-1, 0, 1)
        if abs(dr) < row_tiles and abs(dc) < col_tiles
    ]
    n_slot = len(moves)
    dims = (n_ta, row_tiles, col_tiles, frames_dev, heads, moves)
    vmem = pl.BlockSpec(memory_space=pltpu.VMEM)
    out = jax.ShapeDtypeStruct((rows, width), bf16)
    stat_rows = -(-2 * heads // 8) * 8
    weights = pltpu.VMEM((n_slot, heads, rows, n_ta * rows), f32)
    total = pltpu.VMEM((rows, width), f32)
    dma = pltpu.SemaphoreType.DMA
    results = pl.pallas_call(
        functools.partial(kernel, dims),
        out_shape=(out, out, out),
        in_specs=[pl.BlockSpec(memory_space=pltpu.SMEM)] + [vmem] * 5,
        out_specs=(vmem, vmem, vmem),
        scratch_shapes=[
            pltpu.VMEM((4, n_slot, n_ta, rows, width), bf16),
            pltpu.VMEM((n_slot, n_ta, stat_rows, rows), f32),
            weights,
            weights,
            total,
            total,
            total,
            dma((4, n_slot, n_ta)),
            dma((4, n_slot, n_ta)),
            dma((4, n_ta)),
            dma((4, n_slot, n_ta)),
            dma((n_slot, n_ta)),
            dma((n_slot, n_ta)),
        ],
        compiler_params=pltpu.CompilerParams(
            collective_id=0, has_side_effects=True, vmem_limit_bytes=56 * 1024 * 1024
        ),
    )(
        window_mask.reshape(-1),
        *(x.reshape(rows, width) for x in (query_in, key_in, value_in, saved_out, out_grad)),
    )
    return tuple(x.reshape(shape) for x in results)


def solution(mesh):
    spec = P("ta", "ha", None, None, "ga")
    return jax.shard_map(
        functools.partial(local, mesh.shape["ta"]),
        mesh=mesh,
        in_specs=(spec, spec, spec, spec, spec, P()),
        out_specs=(spec, spec, spec),
        check_vma=False,
    )
```

time: 218 us -> 38.6 us (0.18); the launches traced: 214 us -> 38.4 us
  local copies, waits for them, and re-layouts: 76.3 us -> 4.47 us
  starting transfers between devices: 40.7 us -> 0 us
  Pallas kernels: 0 us -> 33.3 us
  waiting for transfers between devices: 25 us -> 0 us
  matrix products: 24.9 us -> 0 us
  other arithmetic: 17.7 us -> 0 us
  blocking collectives: 15.3 us -> 0 us
  between operations: 14.3 us -> 0.66 us
    ppermute x16 -> x0, starting transfers between devices: 40.6 us -> none  [passed_along(): return lax.ppermute(block, axis, route)]
    pallas_call x0 -> x1, Pallas kernels: none -> 33.3 us  [local(): pl.pallas_call(functools.partial(kernel, dims), out_shape=(out, out, out)...]
    dot_general x6 -> x0, matrix products: 24.9 us -> none  [the longest x1 7.63 us: attend(): jnp.einsum('qhd,khd->hqk', grad_rows, value_rows, preferred_element_type=...]
    reshape x6 -> x1, local copies, waits for them, and re-layouts: 17.6 us -> 0.65 us  [local(): window_mask.reshape(-1)]
    squeeze x8 -> x0, local copies, waits for them, and re-layouts: 16 us -> none  [the longest x4 8.01 us: local(): key_block[place_index]]
    reduce_scatter x2 -> x0, waiting for transfers between devices: 15.3 us -> none  [the longest x1 15.3 us: local(): lax.psum_scatter(key_sum, 'ta', scatter_dimension=0, tiled=True)]
    all_gather x2 -> x0, blocking collectives: 15.3 us -> none  [the longest x1 8.14 us: local(): lax.all_gather(own_pair[1], 'ta', axis=0, tiled=True)]
    slice x8 -> x0, local copies, waits for them, and re-layouts: 15.3 us -> none  [the longest x4 7.67 us: local(): key_block[place_index]]
  transfers between devices with their start and end apart: 18 -> 0, of which waited for: 2 -> 0; matrix products, arithmetic and copies ran while one was open for 53% -> 0% of each run, Pallas kernels for 0% -> 0%
where the time goes in v1:
time: 38.6 us; the launch traced here: 38.4 us
  Pallas kernels  33.3 us (86%)
  local copies, waits for them, and re-layouts  4.47 us (12%)
  between operations  0.66 us (2%)
    pallas_call x1, Pallas kernels, local(): pl.pallas_call(functools.partial(kernel, dims), out_shape=(out, out, out)...  33.3 us
    unnamed x9, local copies, waits for them, and re-layouts  3.83 us

profile of v1, /device:TPU:9, one launch (start us, length us, event | category | flops | bytes accessed | tf_op | source)
XLA Modules:
  0.0 38.4 jit_solution(14172645622129965170)
XLA Ops:
  0.6 0.0 copy-start.2
  0.6 0.7 %copy-done.2 = s32[2,1,4,27]{3,2,1,0:T(4,128)S(1)} copy-done((s32[2,1,4,27]{3,2,1,0:T(4,128)S(1)}, s32[2,1,4,27]{3,2,1,0:T(4,128)}, u32[]{:S(2)}) %copy-start.2) | copy-done | bytes 888
  1.3 0.6 %reshape.33.mask_ref = s32[216]{0:T(256)} reshape(s32[2,1,4,27]{3,2,1,0:T(4,128)S(1)} %copy-done.2) | data formatting | bytes 1728 | tf_op jit(solution)/shard_map/reshape | solution.py:421
  2.0 33.3 %shard_map.85 = (bf16[192,256]{1,0:T(8,128)(2,1)}, bf16[192,256]{1,0:T(8,128)(2,1)}, bf16[192,256]{1,0:T(8,128)(2,1)}) custom-call(s32[216]{0:T(256)} %reshape.33.mask_ref, bf16[192,256]{1,0:T(8,128)(2,1)} %bitcast.17, bf16[192,256]{1,0:T(8,128)(2,1)} %bitcast.18, bf16[192,256]{1,0:T(8,128)(2,1)} %bitcast.19, bf16[192,256]{1,0:T(8,128)(2,1)} %bitcast.20, ...), custom_call_target="tpu_custom_call" | custom-call | tf_op jit(solution)/shard_map/pallas_call | solution.py:397
  35.2 0.0 copy-start.1
  35.3 1.6 %copy.15 = bf16[3,1,8,8,256]{4,3,2,1,0:T(8,128)(2,1)} copy(bf16[3,1,8,8,256]{4,3,2,1,0:T(8,128)(2,1)} %bitcast.16) | data formatting | bytes 196608
  36.8 0.0 copy-done.1
  36.8 0.0 copy-start
  36.8 0.6 %copy.16 = bf16[3,1,8,8,256]{4,3,2,1,0:T(8,128)(2,1)} copy(bf16[3,1,8,8,256]{4,3,2,1,0:T(8,128)(2,1)S(1)} %bitcast.15) | data formatting | bytes 196608
  37.5 0.3 copy-done
  37.8 0.6 %copy.17 = bf16[3,1,8,8,256]{4,3,2,1,0:T(8,128)(2,1)} copy(bf16[3,1,8,8,256]{4,3,2,1,0:T(8,128)(2,1)S(1)} %bitcast.14) | data formatting | bytes 196608
Async XLA Ops:
  0.6 0.7 %copy-start.2 = (s32[2,1,4,27]{3,2,1,0:T(4,128)S(1)}, s32[2,1,4,27]{3,2,1,0:T(4,128)}, u32[]{:S(2)}) copy-start(s32[2,1,4,27]{3,2,1,0:T(4,128)} %param.11) | copy-start | bytes 2596
  35.2 1.6 %copy-start.1 = (bf16[192,256]{1,0:T(8,128)(2,1)S(1)}, bf16[192,256]{1,0:T(8,128)(2,1)}, u32[]{:S(2)}) copy-start(bf16[192,256]{1,0:T(8,128)(2,1)} %get-tuple-element.7) | copy-start | bytes 294916
  36.8 0.9 %copy-start = (bf16[192,256]{1,0:T(8,128)(2,1)S(1)}, bf16[192,256]{1,0:T(8,128)(2,1)}, u32[]{:S(2)}) copy-start(bf16[192,256]{1,0:T(8,128)(2,1)} %get-tuple-element.8) | copy-start | bytes 294916

commit v2 on v1

--- a/solution.py
+++ b/solution.py
@@ -13,6 +13,7 @@
 LOWEST = -1e30
 MESH = pl.DeviceIdType.MESH
 KEY, QUERY, GRAD, VALUE = range(4)
+ACROSS_SPAN = (QUERY,)
 
 
 def kernel(
@@ -33,6 +34,8 @@
     dq_acc,
     dk_acc,
     dv_acc,
+    saved,
+    load_sem,
     pair_sem,
     plane_sem,
     span_sem,
@@ -42,12 +45,14 @@
 ):
     f32, bf16 = jnp.float32, jnp.bfloat16
     n_ta, row_tiles, col_tiles, frames_dev, heads, moves = dims
-    rows = q_ref.shape[0]
+    rows = saved.shape[0]
     n_slot = len(moves)
     centre = moves.index((0, 0))
     others = [s for s in range(n_slot) if s != centre]
     order = [centre] + others
     keys = n_ta * rows
+    step = 256 if keys % 256 == 0 else keys
+    chunks = [slice(at, at + step) for at in range(0, keys, step)]
     scale = HEAD_DIM ** (-0.5)
     to_two = scale * LOG2_E
     n_low = 2 if n_ta % 2 == 0 else 1
@@ -97,9 +102,14 @@
         j = (high + d) % n_high * n_low + low
         return near.at[a, s, j], j
 
-    def span_copy(a, d):
+    def span_copy(a, s, d):
+        src, _ = held(a, s, 0)
         j = (high + d) % n_high * n_low + low
-        return push(own[a], a, centre, time, span_sem.at[a, d], (j, plane, group))
+        return push(src, a, s, time, span_sem.at[a, s, d], (j, plane, group))
+
+    def start_span(a, s):
+        for d in range(1, n_high):
+            span_copy(a, s, d).start()
 
     def plane_copy(a, s, d):
         src, j = held(a, centre, d)
@@ -114,10 +124,8 @@
         block = near.at[a, s, j]
         push(block, a, s, j, recv_sem.at[a, s, j], (time, plane, group)).wait_recv()
 
-    def wait_chain(a, s):
-        for d in range(n_high):
-            if s != centre or d != 0:
-                arrived(a, s, (high + d) % n_high * n_low + low)
+    def chain_arrived(a, s, d):
+        arrived(a, s, (high + d) % n_high * n_low + low)
 
     def wait_pair(a, s):
         if n_low == 2:
@@ -133,20 +141,20 @@
             if_inside(s, lambda s=s: plane_copy(a, s, d).start())
 
     def pass_on_span(a):
-        wait_chain(a, centre)
         for d in range(1, n_high):
-            start_planes(a, d)
+            chain_arrived(a, centre, d)
+            if a not in ACROSS_SPAN:
+                start_planes(a, d)
             start_pair(a, centre, d)
 
-    def pass_on_planes(a):
-        for s in others:
-
-            def do(s=s):
-                wait_chain(a, s)
-                for d in range(n_high):
-                    start_pair(a, s, d)
-
-            if_inside(s, do)
+    def pass_on_planes(a, s, d):
+        def do():
+            chain_arrived(a, s, d)
+            if a in ACROSS_SPAN and d == 0:
+                start_span(a, s)
+            start_pair(a, s, d)
+
+        if_inside(s, do)
 
     def wait_rest(a, s):
         if_inside(s, lambda: wait_pair(a, s))
@@ -179,6 +187,13 @@
             else:
                 pl.when(inside[s])(functools.partial(do, s, j))
 
+    loads = [
+        pltpu.make_async_copy(own[a], near.at[a, centre, time], load_sem.at[a])
+        for a in (KEY, QUERY, GRAD, VALUE)
+    ] + [pltpu.make_async_copy(o_ref, saved, load_sem.at[4])]
+    for load in loads:
+        load.start()
+
     barrier = pltpu.get_barrier_semaphore()
 
     def greet(s, j):
@@ -191,16 +206,11 @@
     planes = sum(jnp.where(inside[s], 1, 0) for s in range(n_slot))
     pl.semaphore_wait(barrier, planes * n_ta - 1)
 
-    for a in (KEY, QUERY, GRAD, VALUE):
-        for d in range(1, n_high):
-            span_copy(a, d).start()
-        if a == KEY:
-            start_planes(a, 0)
-    for a in (KEY, QUERY, GRAD, VALUE):
+    start_planes(KEY, 0)
+    for a in (KEY, VALUE, QUERY, GRAD):
+        start_span(a, centre)
         start_pair(a, centre, 0)
 
-    for a in (KEY, QUERY, GRAD, VALUE):
-        near[a, centre, time] = own[a][...]
     for s in others:
 
         @pl.when(jnp.logical_not(inside[s]))
@@ -209,15 +219,20 @@
                 near[a, s] = jnp.zeros(near.shape[2:], bf16)
             stats[s] = jnp.zeros(stats.shape[1:], f32)
 
+    for load in loads:
+        load.wait()
+
     head_of = [slice(h * HEAD_DIM, (h + 1) * HEAD_DIM) for h in range(heads)]
     column = lax.broadcasted_iota(jnp.int32, (1, keys), 1)
+    def mine(a, h):
+        return near[a, centre, time, :, head_of[h]]
+
     row_dot = [
         jnp.sum(
-            g_ref[:, head_of[h]].astype(f32) * o_ref[:, head_of[h]].astype(f32),
+            mine(GRAD, h).astype(f32) * saved[:, head_of[h]].astype(f32),
             axis=-1,
             keepdims=True,
         )
-        * scale
         for h in range(heads)
     ]
 
@@ -238,8 +253,7 @@
                 row_step, col_step = -dr, -dc
             close = (time_step >= -1) & (time_step <= 1)
             code = (jnp.clip(time_step, -1, 1) + 1) * 9 + (row_step + 1) * 3 + (col_step + 1)
-            tile = (query_time * row_tiles + query_row) * col_tiles + query_col
-            is_open = (mask_ref[tile * 27 + code] == 1) & close & inside[s]
+            is_open = (mask_ref[query_time, query_row, query_col, code] == 1) & close & inside[s]
             here = (column >= j * rows) & (column < (j + 1) * rows)
             bias = jnp.where(here & is_open, 0.0, bias)
         return bias
@@ -253,28 +267,43 @@
     slot_max = {}
     slot_sum = {}
 
+    def fold(values, combine):
+        parts = [values[:, at : at + 128] for at in range(0, step, 128)]
+        return functools.reduce(combine, parts)
+
     def own_scores(s):
         bias = open_bias(s, True)
         for h in range(heads):
-            scores = dot(q_ref[:, head_of[h]], block_of(KEY, s, h), ((1,), (1,))) + bias
-            top = jnp.maximum(jnp.max(scores, axis=-1, keepdims=True), LOWEST)
-            lifted = jnp.exp2((scores - top) * to_two)
-            raised[s, h] = lifted
+            query, near_keys = mine(QUERY, h), block_of(KEY, s, h)
+            tops = []
+            for c in chunks:
+                scores = dot(query, near_keys[c], ((1,), (1,))) + bias[:, c]
+                raised[s, h, :, c] = scores
+                tops.append(fold(scores, jnp.maximum))
+            top = functools.reduce(jnp.maximum, tops)
+            top = jnp.maximum(jnp.max(top, axis=-1, keepdims=True), LOWEST)
+            sums = []
+            for c in chunks:
+                lifted = jnp.exp2((raised[s, h, :, c] - top) * to_two)
+                raised[s, h, :, c] = lifted
+                sums.append(fold(lifted, jnp.add))
+            total = functools.reduce(jnp.add, sums)
             slot_max[s, h] = top
-            slot_sum[s, h] = jnp.sum(lifted, axis=-1, keepdims=True)
+            slot_sum[s, h] = jnp.sum(total, axis=-1, keepdims=True)
 
     pass_on_span(KEY)
+    start_planes(VALUE, 0)
     start_planes(QUERY, 0)
     wait_rest(KEY, centre)
     own_scores(centre)
-    pass_on_span(QUERY)
-    pass_on_planes(KEY)
+    pass_on_span(VALUE)
     start_planes(GRAD, 0)
+    for s in others:
+        for d in range(n_high):
+            pass_on_planes(KEY, s, d)
     for s in others:
         wait_rest(KEY, s)
         own_scores(s)
-    pass_on_span(GRAD)
-    start_planes(VALUE, 0)
 
     factor = {}
     columns = []
@@ -287,7 +316,7 @@
         for s in others:
             total = total + gain[s] * slot_sum[s, h]
         for s in order:
-            factor[s, h] = gain[s] / total
+            factor[s, h] = gain[s] * (scale / total)
         columns.append(top * to_two + jnp.log2(total))
     columns = columns + row_dot
     lane = lax.broadcasted_iota(jnp.int32, (rows, HEAD_DIM), 1)
@@ -297,7 +326,6 @@
     stats[centre, time] = table.T[: stats.shape[2]]
     for s in order:
         each_peer(s, lambda s, j: stat_copy(s, j).start())
-    pass_on_span(VALUE)
 
     def stat_rows(s):
         return jnp.concatenate([stats[s, j] for j in range(n_ta)], axis=1)
@@ -307,8 +335,11 @@
         bias = open_bias(s, False)
         table = stat_rows(s)
         for h in range(heads):
-            scores = dot(k_ref[:, head_of[h]], block_of(QUERY, s, h), ((1,), (1,)))
-            lifted_own[s, h] = jnp.exp2(scores * to_two + (bias - table[h : h + 1]))
+            key, queries = mine(KEY, h), block_of(QUERY, s, h)
+            shift = bias - table[h : h + 1]
+            for c in chunks:
+                scores = dot(key, queries[c], ((1,), (1,)))
+                lifted_own[s, h, :, c] = jnp.exp2(scores * to_two + shift[:, c])
 
     def add(acc, h, first, part):
         if first:
@@ -319,58 +350,83 @@
     def key_grads(s):
         table = stat_rows(s)
         for h in range(heads):
-            grads = block_of(GRAD, s, h)
-            weights = lifted_own[s, h]
-            add(dv_acc, h, s == centre, dot(weights.astype(bf16), grads, ((1,), (0,))))
-            weight_grad = dot(v_ref[:, head_of[h]], grads, ((1,), (1,)))
+            grads, queries, value = block_of(GRAD, s, h), block_of(QUERY, s, h), mine(VALUE, h)
             shift = table[heads + h : heads + h + 1]
-            score_grad = (weights * (weight_grad * scale - shift)).astype(bf16)
-            part = dot(score_grad, block_of(QUERY, s, h), ((1,), (0,)))
-            add(dk_acc, h, s == centre, part)
+            value_part = key_part = 0.0
+            for c in chunks:
+                weights = lifted_own[s, h, :, c]
+                value_part += dot(weights.astype(bf16), grads[c], ((1,), (0,)))
+                weight_grad = dot(value, grads[c], ((1,), (1,)))
+                score_grad = (weights * (weight_grad - shift[:, c])).astype(bf16)
+                key_part += dot(score_grad, queries[c], ((1,), (0,)))
+            add(dv_acc, h, s == centre, value_part)
+            add(dk_acc, h, s == centre, key_part)
 
     def query_grads(s):
         for h in range(heads):
-            weight_grad = dot(g_ref[:, head_of[h]], block_of(VALUE, s, h), ((1,), (1,)))
-            weights = raised[s, h] * factor[s, h]
-            score_grad = (weights * (weight_grad * scale - row_dot[h])).astype(bf16)
-            part = dot(score_grad, block_of(KEY, s, h), ((1,), (0,)))
-            add(dq_acc, h, s == centre, part)
-
-    pass_on_planes(QUERY)
-    for s in order:
-        wait_rest(QUERY, s)
-        key_weights(s)
+            grad, values, near_keys = mine(GRAD, h), block_of(VALUE, s, h), block_of(KEY, s, h)
+            query_part = 0.0
+            for c in chunks:
+                weight_grad = dot(grad, values[c], ((1,), (1,)))
+                score_grad = (raised[s, h, :, c] * (weight_grad - row_dot[h])).astype(bf16)
+                query_part += dot(score_grad, near_keys[c], ((1,), (0,)))
+            add(dq_acc, h, s == centre, query_part * factor[s, h])
+
+    pass_on_span(QUERY)
+    pass_on_span(GRAD)
+    wait_rest(VALUE, centre)
+    query_grads(centre)
+    for a in (VALUE, QUERY):
+        for s in others:
+            pass_on_planes(a, s, 0)
+    wait_rest(QUERY, centre)
+    key_weights(centre)
     wait_rest(GRAD, centre)
     key_grads(centre)
-    wait_rest(VALUE, centre)
-    query_grads(centre)
-    pass_on_planes(GRAD)
-    for s in others:
-        wait_rest(GRAD, s)
-        key_grads(s)
-    pass_on_planes(VALUE)
-    dk_ref[...] = dk_acc[...].astype(bf16)
-    dv_ref[...] = dv_acc[...].astype(bf16)
+    for s in others:
+        for d in range(1, n_high):
+            pass_on_planes(VALUE, s, d)
     for s in others:
         wait_rest(VALUE, s)
         query_grads(s)
     dq_ref[...] = dq_acc[...].astype(bf16)
+    for s in others:
+        pass_on_planes(GRAD, s, 0)
+        for d in range(1, n_high):
+            pass_on_planes(QUERY, s, d)
+    for s in others:
+        wait_rest(QUERY, s)
+        key_weights(s)
+    for s in others:
+        for d in range(1, n_high):
+            pass_on_planes(GRAD, s, d)
+    for s in others:
+        wait_rest(GRAD, s)
+        key_grads(s)
+    dk_ref[...] = (dk_acc[...] * scale).astype(bf16)
+    dv_ref[...] = dv_acc[...].astype(bf16)
 
     for a in (KEY, QUERY, GRAD, VALUE):
-        for d in range(1, n_high):
-            span_copy(a, d).wait_send()
         for s in order:
 
             def finish(s=s, a=a):
                 for d in range(n_high):
-                    if s != centre:
+                    if s != centre and (d == 0 or a not in ACROSS_SPAN):
                         plane_copy(a, s, d).wait_send()
+                    if d != 0 and (s == centre or a in ACROSS_SPAN):
+                        span_copy(a, s, d).wait_send()
                     if n_low == 2:
                         pair_copy(a, s, d).wait_send()
 
             if_inside(s, finish)
     for s in order:
         each_peer(s, lambda s, j: stat_copy(s, j).wait_send())
+
+
+def write_results(dq_ref, dk_ref, dv_ref, query_grad, key_grad, value_grad):
+    query_grad[...] = dq_ref[...]
+    key_grad[...] = dk_ref[...]
+    value_grad[...] = dv_ref[...]
 
 
 def local(n_ta, query_in, key_in, value_in, saved_out, out_grad, window_mask):
@@ -394,10 +450,11 @@
     weights = pltpu.VMEM((n_slot, heads, rows, n_ta * rows), f32)
     total = pltpu.VMEM((rows, width), f32)
     dma = pltpu.SemaphoreType.DMA
+    kept = pl.BlockSpec(memory_space=pl.ANY)
     results = pl.pallas_call(
         functools.partial(kernel, dims),
         out_shape=(out, out, out),
-        in_specs=[pl.BlockSpec(memory_space=pltpu.SMEM)] + [vmem] * 5,
+        in_specs=[pl.BlockSpec(memory_space=pltpu.SMEM)] + [kept] * 5,
         out_specs=(vmem, vmem, vmem),
         scratch_shapes=[
             pltpu.VMEM((4, n_slot, n_ta, rows, width), bf16),
@@ -407,9 +464,11 @@
             total,
             total,
             total,
+            pltpu.VMEM((rows, width), bf16),
+            dma((5,)),
             dma((4, n_slot, n_ta)),
             dma((4, n_slot, n_ta)),
-            dma((4, n_ta)),
+            dma((4, n_slot, n_ta)),
             dma((4, n_slot, n_ta)),
             dma((n_slot, n_ta)),
             dma((n_slot, n_ta)),
@@ -418,9 +477,15 @@
             collective_id=0, has_side_effects=True, vmem_limit_bytes=56 * 1024 * 1024
         ),
     )(
-        window_mask.reshape(-1),
+        window_mask,
         *(x.reshape(rows, width) for x in (query_in, key_in, value_in, saved_out, out_grad)),
     )
+    results = pl.pallas_call(
+        write_results,
+        out_shape=(out, out, out),
+        in_specs=[vmem] * 3,
+        out_specs=(vmem, vmem, vmem),
+    )(*results)
     return tuple(x.reshape(shape) for x in results)
 
 

time: 38.6 us -> 32.5 us (0.84)
  local copies, waits for them, and re-layouts: 4.47 us -> 0 us
  Pallas kernels: 33.3 us -> 31.4 us
    unnamed x9 -> x0, local copies, waits for them, and re-layouts: 3.83 us -> none
    pallas_call x1, Pallas kernels: 33.3 us -> 29.7 us  [local(): pl.pallas_call(functools.partial(kernel, dims), out_shape=(out, out, out)...]
    pallas_call x0 -> x1, Pallas kernels: none -> 1.7 us  [local(): pl.pallas_call(write_results, out_shape=(out, out, out), in_specs=[vmem]...]
    reshape x1 -> x0, local copies, waits for them, and re-layouts: 0.65 us -> none  [local(): window_mask.reshape(-1)]
where the time goes in v2:
time: 32.5 us; the launch traced here: 32 us
  Pallas kernels  31.4 us (97%)
  between operations  0.64 us (2%)
    pallas_call x1, Pallas kernels, local(): pl.pallas_call(functools.partial(kernel, dims), out_shape=(out, out, out)...  29.7 us
    pallas_call x1, Pallas kernels, local(): pl.pallas_call(write_results, out_shape=(out, out, out), in_specs=[vmem]...  1.7 us

profile of v2, /device:TPU:9, one launch (start us, length us, event | category | flops | bytes accessed | tf_op | source)
XLA Modules:
  0.0 32.0 jit_solution(17074156474128373144)
XLA Ops:
  0.6 29.7 %shard_map.85 = (bf16[192,256]{1,0:T(8,128)(2,1)}, bf16[192,256]{1,0:T(8,128)(2,1)}, bf16[192,256]{1,0:T(8,128)(2,1)}) custom-call(s32[2,1,4,27]{3,2,1,0:T(4,128)} %mask_ref.1, bf16[192,256]{1,0:T(8,128)(2,1)} %bitcast.14, bf16[192,256]{1,0:T(8,128)(2,1)} %bitcast.15, bf16[192,256]{1,0:T(8,128)(2,1)} %bitcast.16, bf16[192,256]{1,0:T(8,128)(2,1)} %bitcast.17, ...), custom_call_target="tpu_custom_call" | custom-call | tf_op jit(solution)/shard_map/pallas_call | solution.py:454
  30.3 1.7 %shard_map.86 = (bf16[192,256]{1,0:T(8,128)(2,1)}, bf16[192,256]{1,0:T(8,128)(2,1)}, bf16[192,256]{1,0:T(8,128)(2,1)}) custom-call(bf16[192,256]{1,0:T(8,128)(2,1)} %get-tuple-element.9.dq_ref, bf16[192,256]{1,0:T(8,128)(2,1)} %get-tuple-element.10.dk_ref, bf16[192,256]{1,0:T(8,128)(2,1)} %get-tuple-element.11.dv_ref), custom_call_target="tpu_custom_call" | custom-call | tf_op jit(solution)/shard_map/pallas_call | solution.py:483

commit v3 on v2

--- a/solution.py
+++ b/solution.py
@@ -206,9 +206,9 @@
     planes = sum(jnp.where(inside[s], 1, 0) for s in range(n_slot))
     pl.semaphore_wait(barrier, planes * n_ta - 1)
 
+    start_span(KEY, centre)
     start_planes(KEY, 0)
     for a in (KEY, VALUE, QUERY, GRAD):
-        start_span(a, centre)
         start_pair(a, centre, 0)
 
     for s in others:
@@ -292,18 +292,21 @@
             slot_sum[s, h] = jnp.sum(total, axis=-1, keepdims=True)
 
     pass_on_span(KEY)
+    start_span(VALUE, centre)
+    wait_rest(KEY, centre)
+    own_scores(centre)
     start_planes(VALUE, 0)
     start_planes(QUERY, 0)
-    wait_rest(KEY, centre)
-    own_scores(centre)
-    pass_on_span(VALUE)
-    start_planes(GRAD, 0)
+    start_span(QUERY, centre)
     for s in others:
         for d in range(n_high):
             pass_on_planes(KEY, s, d)
     for s in others:
         wait_rest(KEY, s)
         own_scores(s)
+        if s == others[0]:
+            pass_on_span(VALUE)
+            start_span(GRAD, centre)
 
     factor = {}
     columns = []
@@ -373,12 +376,14 @@
             add(dq_acc, h, s == centre, query_part * factor[s, h])
 
     pass_on_span(QUERY)
-    pass_on_span(GRAD)
+    for s in others:
+        pass_on_planes(QUERY, s, 0)
+    start_planes(GRAD, 0)
     wait_rest(VALUE, centre)
     query_grads(centre)
-    for a in (VALUE, QUERY):
-        for s in others:
-            pass_on_planes(a, s, 0)
+    pass_on_span(GRAD)
+    for s in others:
+        pass_on_planes(VALUE, s, 0)
     wait_rest(QUERY, centre)
     key_weights(centre)
     wait_rest(GRAD, centre)

time: 32.5 us -> 31.6 us (0.972)
  Pallas kernels: 31.4 us -> 30.8 us
    pallas_call x1, Pallas kernels: 29.7 us -> 29.1 us  [local(): pl.pallas_call(functools.partial(kernel, dims), out_shape=(out, out, out)...]
where the time goes in v3:
time: 31.6 us; the launch traced here: 31.4 us
  Pallas kernels  30.8 us (97%)
  between operations  0.64 us (2%)
    pallas_call x1, Pallas kernels, local(): pl.pallas_call(functools.partial(kernel, dims), out_shape=(out, out, out)...  29.1 us
    pallas_call x1, Pallas kernels, local(): pl.pallas_call(write_results, out_shape=(out, out, out), in_specs=[vmem]...  1.7 us

profile of v3, /device:TPU:9, one launch (start us, length us, event | category | flops | bytes accessed | tf_op | source)
XLA Modules:
  0.0 31.4 jit_solution(16827777317735472666)
XLA Ops:
  0.6 29.1 %shard_map.85 = (bf16[192,256]{1,0:T(8,128)(2,1)}, bf16[192,256]{1,0:T(8,128)(2,1)}, bf16[192,256]{1,0:T(8,128)(2,1)}) custom-call(s32[2,1,4,27]{3,2,1,0:T(4,128)} %mask_ref.1, bf16[192,256]{1,0:T(8,128)(2,1)} %bitcast.14, bf16[192,256]{1,0:T(8,128)(2,1)} %bitcast.15, bf16[192,256]{1,0:T(8,128)(2,1)} %bitcast.16, bf16[192,256]{1,0:T(8,128)(2,1)} %bitcast.17, ...), custom_call_target="tpu_custom_call" | custom-call | tf_op jit(solution)/shard_map/pallas_call | solution.py:459
  29.7 1.7 %shard_map.86 = (bf16[192,256]{1,0:T(8,128)(2,1)}, bf16[192,256]{1,0:T(8,128)(2,1)}, bf16[192,256]{1,0:T(8,128)(2,1)}) custom-call(bf16[192,256]{1,0:T(8,128)(2,1)} %get-tuple-element.9.dq_ref, bf16[192,256]{1,0:T(8,128)(2,1)} %get-tuple-element.10.dk_ref, bf16[192,256]{1,0:T(8,128)(2,1)} %get-tuple-element.11.dv_ref), custom_call_target="tpu_custom_call" | custom-call | tf_op jit(solution)/shard_map/pallas_call | solution.py:488

commit v4 on v3

--- a/solution.py
+++ b/solution.py
@@ -36,9 +36,8 @@
     dv_acc,
     saved,
     load_sem,
+    sent,
     pair_sem,
-    plane_sem,
-    span_sem,
     recv_sem,
     stat_send,
     stat_recv,
@@ -86,109 +85,118 @@
         else:
             pl.when(inside[s])(do)
 
-    def push(src, a, s, j, send_sem, device):
+    def place_of(t):
+        return t % n_low * n_high + t // n_low
+
+    def time_of(p):
+        return p % n_high * n_low + p // n_high
+
+    here = place_of(time)
+    chain = low * n_high
+    across = (1 - low) * n_high
+
+    def push(src, dst, send_sem, recv_sem, device):
         return pltpu.make_async_remote_copy(
             src_ref=src,
-            dst_ref=near.at[a, s, j],
+            dst_ref=dst,
             send_sem=send_sem,
-            recv_sem=recv_sem.at[a, s, j],
+            recv_sem=recv_sem,
             device_id=device,
             device_id_type=MESH,
         )
 
-    def held(a, s, d):
-        if s == centre and d == 0:
-            return own[a], time
-        j = (high + d) % n_high * n_low + low
-        return near.at[a, s, j], j
-
-    def span_copy(a, s, d):
-        src, _ = held(a, s, 0)
-        j = (high + d) % n_high * n_low + low
-        return push(src, a, s, time, span_sem.at[a, s, d], (j, plane, group))
+    def arrival(block, sem):
+        push(block, block, sem, sem, (time, plane, group)).wait_recv()
+
+    def chain_place(d):
+        return chain + (high + d) % n_high
 
     def start_span(a, s):
+        src = own[a] if s == centre else near.at[a, s, here]
         for d in range(1, n_high):
-            span_copy(a, s, d).start()
-
-    def plane_copy(a, s, d):
-        src, j = held(a, centre, d)
-        return push(src, a, back(s), j, plane_sem.at[a, s, d], (time, shifted(s), group))
-
-    def pair_copy(a, s, d):
-        src, j = held(a, s, d)
-        partner = high * n_low + 1 - low
-        return push(src, a, s, j, pair_sem.at[a, s, d], (partner, plane, group))
-
-    def arrived(a, s, j):
-        block = near.at[a, s, j]
-        push(block, a, s, j, recv_sem.at[a, s, j], (time, plane, group)).wait_recv()
+            j = (high + d) % n_high * n_low + low
+            push(
+                src, near.at[a, s, here], sent.at[a, s], recv_sem.at[a, s, here], (j, plane, group)
+            ).start()
+
+    def start_planes(a, d):
+        p = chain_place(d)
+        src = own[a] if d == 0 else near.at[a, centre, p]
+        for s in others:
+
+            @pl.when(inside[s])
+            def _(s=s):
+                device = (time, shifted(s), group)
+                r = back(s)
+                push(
+                    src, near.at[a, r, p], sent.at[a, s], recv_sem.at[a, r, p], device
+                ).start()
+
+    def start_pair(a, s, src, dst):
+        if n_low == 2:
+            device = (high * n_low + 1 - low, plane, group)
+            push(src, dst, sent.at[a, s], pair_sem.at[a, s], device).start()
 
     def chain_arrived(a, s, d):
-        arrived(a, s, (high + d) % n_high * n_low + low)
-
-    def wait_pair(a, s):
-        if n_low == 2:
-            for h in range(n_high):
-                arrived(a, s, h * n_low + 1 - low)
-
-    def start_pair(a, s, d):
-        if n_low == 2:
-            pair_copy(a, s, d).start()
-
-    def start_planes(a, d):
-        for s in others:
-            if_inside(s, lambda s=s: plane_copy(a, s, d).start())
+        p = chain_place(d)
+        arrival(near.at[a, s, p], recv_sem.at[a, s, p])
 
     def pass_on_span(a):
         for d in range(1, n_high):
             chain_arrived(a, centre, d)
             if a not in ACROSS_SPAN:
                 start_planes(a, d)
-            start_pair(a, centre, d)
-
-    def pass_on_planes(a, s, d):
+            block = near.at[a, centre, chain_place(d)]
+            start_pair(a, centre, block, block)
+
+    def span_planes(a):
+        for s in others:
+
+            @pl.when(inside[s])
+            def _(s=s):
+                chain_arrived(a, s, 0)
+                start_span(a, s)
+
+    def pass_on_planes(a):
+        for s in others:
+
+            @pl.when(inside[s])
+            def _(s=s):
+                for d in range(n_high):
+                    if d != 0 or a not in ACROSS_SPAN:
+                        chain_arrived(a, s, d)
+                blocks = near.at[a, s, pl.ds(chain, n_high)]
+                start_pair(a, s, blocks, blocks)
+
+    def wait_rest(a, s):
+        if n_low == 2:
+            if_inside(
+                s, lambda: arrival(near.at[a, s, pl.ds(across, n_high)], pair_sem.at[a, s])
+            )
+
+    def peers(s):
+        if s == centre:
+            return [(time + d) % n_ta for d in range(1, n_ta)]
+        return list(range(n_ta))
+
+    def send_stats(s):
         def do():
-            chain_arrived(a, s, d)
-            if a in ACROSS_SPAN and d == 0:
-                start_span(a, s)
-            start_pair(a, s, d)
+            for j in peers(s):
+                push(
+                    stats.at[centre, here],
+                    stats.at[back(s), here],
+                    stat_send.at[s],
+                    stat_recv.at[back(s)],
+                    (j, shifted(s), group),
+                ).start()
 
         if_inside(s, do)
 
-    def wait_rest(a, s):
-        if_inside(s, lambda: wait_pair(a, s))
-
-    def stat_copy(s, j):
-        return pltpu.make_async_remote_copy(
-            src_ref=stats.at[centre, time],
-            dst_ref=stats.at[back(s), time],
-            send_sem=stat_send.at[s, j],
-            recv_sem=stat_recv.at[back(s), time],
-            device_id=(j, shifted(s), group),
-            device_id_type=MESH,
-        )
-
-    def stat_arrived(s, j):
-        block = stats.at[s, j]
-        pltpu.make_async_remote_copy(
-            src_ref=block,
-            dst_ref=block,
-            send_sem=stat_send.at[s, j],
-            recv_sem=stat_recv.at[s, j],
-            device_id=(time, plane, group),
-            device_id_type=MESH,
-        ).wait_recv()
-
-    def each_peer(s, do):
-        for j in range(n_ta):
-            if s == centre:
-                pl.when(time != j)(functools.partial(do, s, j))
-            else:
-                pl.when(inside[s])(functools.partial(do, s, j))
+    def stats_of(s):
+        return stats.at[s, pl.ds(0, len(peers(s)))]
 
     loads = [
-        pltpu.make_async_copy(own[a], near.at[a, centre, time], load_sem.at[a])
+        pltpu.make_async_copy(own[a], near.at[a, centre, here], load_sem.at[a])
         for a in (KEY, QUERY, GRAD, VALUE)
     ] + [pltpu.make_async_copy(o_ref, saved, load_sem.at[4])]
     for load in loads:
@@ -196,20 +204,21 @@
 
     barrier = pltpu.get_barrier_semaphore()
 
-    def greet(s, j):
-        pl.semaphore_signal(
-            barrier, inc=1, device_id=(j, shifted(s), group), device_id_type=MESH
-        )
+    def greet(s):
+        for j in peers(s):
+            pl.semaphore_signal(
+                barrier, inc=1, device_id=(j, shifted(s), group), device_id_type=MESH
+            )
 
     for s in order:
-        each_peer(s, greet)
+        if_inside(s, functools.partial(greet, s))
     planes = sum(jnp.where(inside[s], 1, 0) for s in range(n_slot))
     pl.semaphore_wait(barrier, planes * n_ta - 1)
 
     start_span(KEY, centre)
     start_planes(KEY, 0)
     for a in (KEY, VALUE, QUERY, GRAD):
-        start_pair(a, centre, 0)
+        start_pair(a, centre, own[a], near.at[a, centre, here])
 
     for s in others:
 
@@ -224,8 +233,9 @@
 
     head_of = [slice(h * HEAD_DIM, (h + 1) * HEAD_DIM) for h in range(heads)]
     column = lax.broadcasted_iota(jnp.int32, (1, keys), 1)
+
     def mine(a, h):
-        return near[a, centre, time, :, head_of[h]]
+        return near[a, centre, here, :, head_of[h]]
 
     row_dot = [
         jnp.sum(
@@ -242,7 +252,8 @@
     def open_bias(s, as_query):
         dr, dc = moves[s]
         bias = jnp.full((1, keys), -jnp.inf, f32)
-        for j in range(n_ta):
+        for p in range(n_ta):
+            j = time_of(p)
             if as_query:
                 query_time, time_step = tile_time(time), tile_time(j) - tile_time(time)
                 query_row, query_col, row_step, col_step = row_tile, col_tile, dr, dc
@@ -254,8 +265,8 @@
             close = (time_step >= -1) & (time_step <= 1)
             code = (jnp.clip(time_step, -1, 1) + 1) * 9 + (row_step + 1) * 3 + (col_step + 1)
             is_open = (mask_ref[query_time, query_row, query_col, code] == 1) & close & inside[s]
-            here = (column >= j * rows) & (column < (j + 1) * rows)
-            bias = jnp.where(here & is_open, 0.0, bias)
+            block = (column >= p * rows) & (column < (p + 1) * rows)
+            bias = jnp.where(block & is_open, 0.0, bias)
         return bias
 
     def dot(a, b, dims):
@@ -298,9 +309,7 @@
     start_planes(VALUE, 0)
     start_planes(QUERY, 0)
     start_span(QUERY, centre)
-    for s in others:
-        for d in range(n_high):
-            pass_on_planes(KEY, s, d)
+    pass_on_planes(KEY)
     for s in others:
         wait_rest(KEY, s)
         own_scores(s)
@@ -326,15 +335,14 @@
     table = jnp.zeros((rows, HEAD_DIM), f32)
     for index, col in enumerate(columns):
         table = jnp.where(lane == index, col, table)
-    stats[centre, time] = table.T[: stats.shape[2]]
+    stats[centre, here] = table.T[: stats.shape[2]]
     for s in order:
-        each_peer(s, lambda s, j: stat_copy(s, j).start())
+        send_stats(s)
 
     def stat_rows(s):
         return jnp.concatenate([stats[s, j] for j in range(n_ta)], axis=1)
 
     def key_weights(s):
-        each_peer(s, stat_arrived)
         bias = open_bias(s, False)
         table = stat_rows(s)
         for h in range(heads):
@@ -375,57 +383,52 @@
                 query_part += dot(score_grad, near_keys[c], ((1,), (0,)))
             add(dq_acc, h, s == centre, query_part * factor[s, h])
 
+    def wait_stats(s):
+        if_inside(s, lambda: arrival(stats_of(s), stat_recv.at[s]))
+
     pass_on_span(QUERY)
-    for s in others:
-        pass_on_planes(QUERY, s, 0)
+    span_planes(QUERY)
     start_planes(GRAD, 0)
     wait_rest(VALUE, centre)
     query_grads(centre)
     pass_on_span(GRAD)
-    for s in others:
-        pass_on_planes(VALUE, s, 0)
+    pass_on_planes(VALUE)
     wait_rest(QUERY, centre)
+    wait_rest(GRAD, centre)
+    wait_stats(centre)
     key_weights(centre)
-    wait_rest(GRAD, centre)
     key_grads(centre)
     for s in others:
-        for d in range(1, n_high):
-            pass_on_planes(VALUE, s, d)
-    for s in others:
         wait_rest(VALUE, s)
+    for s in others:
         query_grads(s)
     dq_ref[...] = dq_acc[...].astype(bf16)
-    for s in others:
-        pass_on_planes(GRAD, s, 0)
-        for d in range(1, n_high):
-            pass_on_planes(QUERY, s, d)
+    pass_on_planes(QUERY)
     for s in others:
         wait_rest(QUERY, s)
+        wait_stats(s)
+    for s in others:
         key_weights(s)
-    for s in others:
-        for d in range(1, n_high):
-            pass_on_planes(GRAD, s, d)
+    pass_on_planes(GRAD)
     for s in others:
         wait_rest(GRAD, s)
+    for s in others:
         key_grads(s)
     dk_ref[...] = (dk_acc[...] * scale).astype(bf16)
     dv_ref[...] = dv_acc[...].astype(bf16)
 
-    for a in (KEY, QUERY, GRAD, VALUE):
-        for s in order:
-
-            def finish(s=s, a=a):
-                for d in range(n_high):
-                    if s != centre and (d == 0 or a not in ACROSS_SPAN):
-                        plane_copy(a, s, d).wait_send()
-                    if d != 0 and (s == centre or a in ACROSS_SPAN):
-                        span_copy(a, s, d).wait_send()
-                    if n_low == 2:
-                        pair_copy(a, s, d).wait_send()
-
-            if_inside(s, finish)
+    def all_sent(s):
+        count = (n_high if n_low == 1 else n_ta) - (1 if s == centre else 0)
+        for a in (KEY, QUERY, GRAD, VALUE):
+            block = near.at[a, s, pl.ds(0, count)]
+            push(block, block, sent.at[a, s], sent.at[a, s], (time, plane, group)).wait_send()
+        block = stats_of(s)
+        push(
+            block, block, stat_send.at[s], stat_send.at[s], (time, plane, group)
+        ).wait_send()
+
     for s in order:
-        each_peer(s, lambda s, j: stat_copy(s, j).wait_send())
+        if_inside(s, functools.partial(all_sent, s))
 
 
 def write_results(dq_ref, dk_ref, dv_ref, query_grad, key_grad, value_grad):
@@ -471,12 +474,11 @@
             total,
             pltpu.VMEM((rows, width), bf16),
             dma((5,)),
+            dma((4, n_slot)),
+            dma((4, n_slot)),
             dma((4, n_slot, n_ta)),
-            dma((4, n_slot, n_ta)),
-            dma((4, n_slot, n_ta)),
-            dma((4, n_slot, n_ta)),
-            dma((n_slot, n_ta)),
-            dma((n_slot, n_ta)),
+            dma((n_slot,)),
+            dma((n_slot,)),
         ],
         compiler_params=pltpu.CompilerParams(
             collective_id=0, has_side_effects=True, vmem_limit_bytes=56 * 1024 * 1024

time: 31.6 us -> 30.9 us (0.978)
  Pallas kernels: 30.8 us -> 30.1 us
    pallas_call x1, Pallas kernels: 29.1 us -> 28.4 us  [local(): pl.pallas_call(functools.partial(kernel, dims), out_shape=(out, out, out)...]
where the time goes in v4:
time: 30.9 us; the launch traced here: 30.7 us
  Pallas kernels  30.1 us (97%)
  between operations  0.64 us (2%)
    pallas_call x1, Pallas kernels, local(): pl.pallas_call(functools.partial(kernel, dims), out_shape=(out, out, out)...  28.4 us
    pallas_call x1, Pallas kernels, local(): pl.pallas_call(write_results, out_shape=(out, out, out), in_specs=[vmem]...  1.7 us

profile of v4, /device:TPU:9, one launch (start us, length us, event | category | flops | bytes accessed | tf_op | source)
XLA Modules:
  0.0 30.7 jit_solution(15269495106618483092)
XLA Ops:
  0.6 28.4 %shard_map.85 = (bf16[192,256]{1,0:T(8,128)(2,1)}, bf16[192,256]{1,0:T(8,128)(2,1)}, bf16[192,256]{1,0:T(8,128)(2,1)}) custom-call(s32[2,1,4,27]{3,2,1,0:T(4,128)} %mask_ref.1, bf16[192,256]{1,0:T(8,128)(2,1)} %bitcast.14, bf16[192,256]{1,0:T(8,128)(2,1)} %bitcast.15, bf16[192,256]{1,0:T(8,128)(2,1)} %bitcast.16, bf16[192,256]{1,0:T(8,128)(2,1)} %bitcast.17, ...), custom_call_target="tpu_custom_call" | custom-call | tf_op jit(solution)/shard_map/pallas_call | solution.py:462
  29.0 1.7 %shard_map.86 = (bf16[192,256]{1,0:T(8,128)(2,1)}, bf16[192,256]{1,0:T(8,128)(2,1)}, bf16[192,256]{1,0:T(8,128)(2,1)}) custom-call(bf16[192,256]{1,0:T(8,128)(2,1)} %get-tuple-element.9.dq_ref, bf16[192,256]{1,0:T(8,128)(2,1)} %get-tuple-element.10.dk_ref, bf16[192,256]{1,0:T(8,128)(2,1)} %get-tuple-element.11.dv_ref), custom_call_target="tpu_custom_call" | custom-call | tf_op jit(solution)/shard_map/pallas_call | solution.py:490

commit v5 on v4

--- a/solution.py
+++ b/solution.py
@@ -316,6 +316,7 @@
         if s == others[0]:
             pass_on_span(VALUE)
             start_span(GRAD, centre)
+            start_planes(GRAD, 0)
 
     factor = {}
     columns = []
@@ -388,10 +389,9 @@
 
     pass_on_span(QUERY)
     span_planes(QUERY)
-    start_planes(GRAD, 0)
+    pass_on_span(GRAD)
     wait_rest(VALUE, centre)
     query_grads(centre)
-    pass_on_span(GRAD)
     pass_on_planes(VALUE)
     wait_rest(QUERY, centre)
     wait_rest(GRAD, centre)
@@ -400,16 +400,16 @@
     key_grads(centre)
     for s in others:
         wait_rest(VALUE, s)
-    for s in others:
         query_grads(s)
+        if s == others[0]:
+            pass_on_planes(QUERY)
     dq_ref[...] = dq_acc[...].astype(bf16)
-    pass_on_planes(QUERY)
+    pass_on_planes(GRAD)
     for s in others:
         wait_rest(QUERY, s)
         wait_stats(s)
     for s in others:
         key_weights(s)
-    pass_on_planes(GRAD)
     for s in others:
         wait_rest(GRAD, s)
     for s in others:

time: 30.9 us -> 30.4 us (0.984)
  Pallas kernels: 30.1 us -> 29.6 us
    pallas_call x1, Pallas kernels: 28.4 us -> 27.9 us  [local(): pl.pallas_call(functools.partial(kernel, dims), out_shape=(out, out, out)...]
where the time goes in v5:
time: 30.4 us; the launch traced here: 30.2 us
  Pallas kernels  29.6 us (97%)
  between operations  0.64 us (2%)
    pallas_call x1, Pallas kernels, local(): pl.pallas_call(functools.partial(kernel, dims), out_shape=(out, out, out)...  27.9 us
    pallas_call x1, Pallas kernels, local(): pl.pallas_call(write_results, out_shape=(out, out, out), in_specs=[vmem]...  1.7 us

profile of v5, /device:TPU:9, one launch (start us, length us, event | category | flops | bytes accessed | tf_op | source)
XLA Modules:
  0.0 30.2 jit_solution(14207606108282892597)
XLA Ops:
  0.6 27.9 %shard_map.85 = (bf16[192,256]{1,0:T(8,128)(2,1)}, bf16[192,256]{1,0:T(8,128)(2,1)}, bf16[192,256]{1,0:T(8,128)(2,1)}) custom-call(s32[2,1,4,27]{3,2,1,0:T(4,128)} %mask_ref.1, bf16[192,256]{1,0:T(8,128)(2,1)} %bitcast.14, bf16[192,256]{1,0:T(8,128)(2,1)} %bitcast.15, bf16[192,256]{1,0:T(8,128)(2,1)} %bitcast.16, bf16[192,256]{1,0:T(8,128)(2,1)} %bitcast.17, ...), custom_call_target="tpu_custom_call" | custom-call | tf_op jit(solution)/shard_map/pallas_call | solution.py:462
  28.5 1.7 %shard_map.86 = (bf16[192,256]{1,0:T(8,128)(2,1)}, bf16[192,256]{1,0:T(8,128)(2,1)}, bf16[192,256]{1,0:T(8,128)(2,1)}) custom-call(bf16[192,256]{1,0:T(8,128)(2,1)} %get-tuple-element.9.dq_ref, bf16[192,256]{1,0:T(8,128)(2,1)} %get-tuple-element.10.dk_ref, bf16[192,256]{1,0:T(8,128)(2,1)} %get-tuple-element.11.dv_ref), custom_call_target="tpu_custom_call" | custom-call | tf_op jit(solution)/shard_map/pallas_call | solution.py:490
